TPU v7x, 512 devices: a whole 4x4x16 slice. The times are simulated.
512 devices in a mesh: row: 16 (over x, y), col: 32 (over z, core).
Axes of the slice: x: 4, y: 4, z: 16, core: 2. Of those that a mesh axis runs over, the one named last changes fastest.
Arguments:
- tokens: float32 [512, 5120], P('col', 'row'), may hold values from -6 to 6
- w_in: float32 [5120, 20480], P('row', 'col'), may hold values from -0.078125 to 0.078125
- w_out: float32 [20480, 5120], P('col', 'row'), may hold values from -0.0390625 to 0.0390625
- out_grad: float32 [512, 5120], P('col', 'row'), may hold values from -6 to 6
Outputs:
- output: float32 [512, 5120], P('col', 'row')
- in_grad: float32 [512, 5120], P('col', 'row')
- grad_in: float32 [5120, 20480], P('row', 'col')
- grad_out: float32 [20480, 5120], P('col', 'row')
All inputs are finite; a program needn't handle non-finite values.
Results may differ from a plain program's by a relative error of at most 0.000088.
Values sent between devices are 32-bit elements; how exact they have to be, the bound alone decides.
No kernel may reach another device: no remote copies, remote signals or barrier semaphores. Data moves between devices by JAX's collectives and lax.ppermute only.
A program may use at most 64 MiB of HBM per device.

v0:
```python
import math

import jax
import jax.numpy as jnp
from jax import lax
from jax.sharding import PartitionSpec as P


def gelu_parts(hidden):
    coeff = math.sqrt(2.0 / math.pi)
    inner = coeff * (hidden + 0.044715 * hidden * hidden * hidden)
    tangent = jnp.tanh(inner)
    active = 0.5 * hidden * (1.0 + tangent)
    slope = 0.5 * (1.0 + tangent) + 0.5 * hidden * (1.0 - tangent * tangent) * coeff * (
        1.0 + 3.0 * 0.044715 * hidden * hidden
    )
    return (active, slope)


def matmul(left, right):
    return jnp.dot(left, right, preferred_element_type=jnp.float32, precision=lax.Precision.HIGHEST)


def matmul_right_t(left, right):
    return lax.dot_general(
        left,
        right,
        (((1,), (1,)), ((), ())),
        preferred_element_type=jnp.float32,
        precision=lax.Precision.HIGHEST,
    )


def matmul_left_t(left, right):
    return lax.dot_general(
        left,
        right,
        (((0,), (0,)), ((), ())),
        preferred_element_type=jnp.float32,
        precision=lax.Precision.HIGHEST,
    )


def on_device(tokens, w_in, w_out, out_grad):
    gathered_in = lax.all_gather(tokens, "col", axis=0, tiled=True)
    hidden = lax.psum_scatter(matmul(gathered_in, w_in), "row", scatter_dimension=0, tiled=True)
    active, slope = gelu_parts(hidden)
    gathered_act = lax.all_gather(active, "row", axis=0, tiled=True)
    output = lax.psum_scatter(matmul(gathered_act, w_out), "col", scatter_dimension=0, tiled=True)
    gathered_cot = lax.all_gather(out_grad, "col", axis=0, tiled=True)
    grad_out = matmul_left_t(gathered_act, gathered_cot)
    act_grad = lax.psum_scatter(
        matmul_right_t(gathered_cot, w_out), "row", scatter_dimension=0, tiled=True
    )
    hid_grad = act_grad * slope
    gathered_hgrad = lax.all_gather(hid_grad, "row", axis=0, tiled=True)
    grad_in = matmul_left_t(gathered_in, gathered_hgrad)
    in_grad = lax.psum_scatter(
        matmul_right_t(gathered_hgrad, w_in), "col", scatter_dimension=0, tiled=True
    )
    return (output, in_grad, grad_in, grad_out)


def solution(mesh):
    placed = (P("col", "row"), P("row", "col"), P("col", "row"), P("col", "row"))
    return jax.shard_map(
        on_device,
        mesh=mesh,
        in_specs=placed,
        out_specs=(P("col", "row"), P("col", "row"), P("row", "col"), P("col", "row")),
        check_vma=False,
    )
```

profile of v0, /device:TPU:22, one launch (start us, length us, event | category | flops | bytes accessed | tf_op | source)
XLA Modules:
  0.0 576.4 jit_solution(15419062799588617882)
XLA Ops:
  7.2 0.0 reduce-scatter.9.cloned.1.call-start
  7.2 38.8 %all_gather.14 = f32[512,320]{1,0:T(8,128)S(1)} all-gather(f32[16,320]{1,0:T(8,128)} %param.7), channel_id=1, replica_groups=mesh['row'=16,'col'=32] {'col'}, dimensions={0}, use_global_device_ids=true | all-gather | bytes 675840 | tf_op jit(solution)/shard_map/all_gather | solution.py:50
  46.0 3.5 fusion.8
  49.5 0.0 reduce-scatter.5.cloned.1.call-start
  49.6 0.7 copy-done.3
  50.3 29.2 %all_gather.12 = f32[512,320]{1,0:T(8,128)S(1)} all-gather(f32[16,320]{1,0:T(8,128)S(1)} %copy-done.3), channel_id=1, replica_groups=mesh['row'=16,'col'=32] {'col'}, dimensions={0}, use_global_device_ids=true | all-gather | bytes 675840 | tf_op jit(solution)/shard_map/all_gather | solution.py:45
  79.5 3.5 fusion.6
  83.0 0.0 all-gather.3.cloned.1.call-start
  83.0 49.2 %reduce-scatter.9.cloned.1.call-done = f32[32,640]{1,0:T(8,128)} async-done(((f32[512,640]{1,0:T(8,128)}), f32[32,640]{1,0:T(8,128)}) %reduce-scatter.9.cloned.1.call-update) | async-done | bytes 81936 | tf_op jit(solution)/shard_map/reduce_scatter | solution.py:52
  132.2 92.2 %reduce-scatter.5.cloned.1.call-done = f32[32,640]{1,0:T(8,128)} async-done(((f32[512,640]{1,0:T(8,128)}), f32[32,640]{1,0:T(8,128)}) %reduce-scatter.5.cloned.1.call-update) | async-done | bytes 81936 | tf_op jit(solution)/shard_map/reduce_scatter | solution.py:46
  224.4 1.6 fusion.5
  226.1 0.0 all-gather.3.cloned.1.call-update
  226.1 0.0 all-gather.5.cloned.1.call-start
  226.1 0.5 all-gather.5.cloned.1.call-update
  226.7 0.0 reduce-scatter.7.cloned.1.call-start
  226.7 59.5 %all-gather.3.cloned.1.call-done = f32[512,640]{1,0:T(8,128)} async-done(((f32[32,640]{1,0:T(8,128)}), f32[512,640]{1,0:T(8,128)}) %all-gather.3.cloned.1.call-update) | async-done | bytes 1310736 | tf_op jit(solution)/shard_map/all_gather | solution.py:48
  286.2 4.7 fusion.7
  290.9 0.2 reduce-scatter.11.cloned.1.call-start
  291.1 56.7 %all-gather.5.cloned.1.call-done = f32[512,640]{1,0:T(8,128)} async-done(((f32[32,640]{1,0:T(8,128)}), f32[512,640]{1,0:T(8,128)}) %all-gather.5.cloned.1.call-update) | async-done | bytes 1310736 | tf_op jit(solution)/shard_map/all_gather | solution.py:56
  347.9 4.7 fusion.9
  352.6 4.1 fusion.10
  356.7 2.7 convolution_bitcast_fusion
  359.5 101.1 %reduce-scatter.7.cloned.1.call-done = f32[16,320]{1,0:T(8,128)} async-done(((f32[512,320]{1,0:T(8,128)}), f32[16,320]{1,0:T(8,128)}) %reduce-scatter.7.cloned.1.call-update) | async-done | bytes 20496 | tf_op jit(solution)/shard_map/reduce_scatter | solution.py:49
  460.6 109.0 %reduce-scatter.11.cloned.1.call-done = f32[16,320]{1,0:T(8,128)} async-done(((f32[512,320]{1,0:T(8,128)}), f32[16,320]{1,0:T(8,128)}) %reduce-scatter.11.cloned.1.call-update) | async-done | bytes 20496 | tf_op jit(solution)/shard_map/reduce_scatter | solution.py:58
  (11 shorter events, 0.1 us)
Async XLA Ops:
  7.2 38.8 %copy-start = (f32[640,320]{0,1:T(8,128)S(1)}, f32[640,320]{0,1:T(8,128)}, u32[]{:S(2)}) copy-start(f32[640,320]{0,1:T(8,128)} %param.6) | copy-start | bytes 2457604
  7.2 125.0 %reduce-scatter.9.cloned.1.call-start = ((), (), s32[]{:S(2)}) async-start(), calls=%async_computation.7 | async-start | bytes 1392640 | tf_op jit(solution)/shard_map/reduce_scatter | solution.py:52
  49.5 0.7 copy-start.3
  49.5 29.9 %copy-start.2 = (f32[320,640]{1,0:T(8,128)S(1)}, f32[320,640]{1,0:T(8,128)}, u32[]{:S(2)}) copy-start(f32[320,640]{1,0:T(8,128)} %param.5) | copy-start | bytes 2457604
  49.5 174.9 %reduce-scatter.5.cloned.1.call-start = ((), (), s32[]{:S(2)}) async-start(), calls=%async_computation.4 | async-start | bytes 1392640 | tf_op jit(solution)/shard_map/reduce_scatter | solution.py:46
  83.0 203.2 %all-gather.3.cloned.1.call-start = ((), (), s32[]{:S(2)}) async-start(), calls=%async_computation.5 | async-start | bytes 1392640 | tf_op jit(solution)/shard_map/all_gather | solution.py:48
  226.1 121.8 %all-gather.5.cloned.1.call-start = ((), (), s32[]{:S(2)}) async-start(), calls=%async_computation.8 | async-start | bytes 1392640 | tf_op jit(solution)/shard_map/all_gather | solution.py:56
  226.7 233.9 %reduce-scatter.7.cloned.1.call-start = ((), (), s32[]{:S(2)}) async-start(), calls=%async_computation.6 | async-start | bytes 811008 | tf_op jit(solution)/shard_map/reduce_scatter | solution.py:49
  290.9 278.7 %reduce-scatter.11.cloned.1.call-start = ((), (), s32[]{:S(2)}) async-start(), calls=%async_computation.9 | async-start | bytes 811008 | tf_op jit(solution)/shard_map/reduce_scatter | solution.py:58
  352.6 4.2 copy-start.1
Sparse Core Ops, SparseCore 0:
  49.7 82.5 reduce-scatter.8
  136.3 88.0 reduce-scatter.4
  228.1 58.1 all-gather.2
  289.7 58.1 all-gather.4
  351.1 109.4 reduce-scatter.6
  464.0 105.4 reduce-scatter.10
where the time goes:
time: 577 us; the launch traced here: 576 us
  waiting for transfers between devices  468 us (81%)
  blocking collectives  68 us (12%)
  matrix products  23.2 us (4%)
  between operations  14.1 us (2%)
    reduce_scatter x1, waiting for transfers between devices, on_device(): lax.psum_scatter(matmul_right_t(gathered_hgrad, w_in), 'col', scatter_dim...  109 us
    reduce_scatter x1, waiting for transfers between devices, on_device(): lax.psum_scatter(matmul(gathered_act, w_out), 'col', scatter_dimension=0,...  101 us
    reduce_scatter x1, waiting for transfers between devices, on_device(): lax.psum_scatter(matmul(gathered_in, w_in), 'row', scatter_dimension=0, t...  92.2 us
    all_gather x1, waiting for transfers between devices, on_device(): gathered_act = lax.all_gather(active, 'row', axis=0, tiled=True)  59.5 us
    all_gather x1, waiting for transfers between devices, on_device(): gathered_hgrad = lax.all_gather(hid_grad, 'row', axis=0, tiled=True)  56.7 us
    reduce_scatter x1, waiting for transfers between devices, on_device(): lax.psum_scatter(matmul_right_t(gathered_cot, w_out), 'row', scatter_dime...  49.2 us
    all_gather x1, blocking collectives, on_device(): gathered_cot = lax.all_gather(out_grad, 'col', axis=0, tiled=True)  38.8 us
    all_gather x1, blocking collectives, on_device(): gathered_in = lax.all_gather(tokens, 'col', axis=0, tiled=True)  29.2 us
  transfers between devices with their start and end apart: 6, of which 6 were waited for; matrix products, arithmetic and copies ran while one was open for 3% of the time, Pallas kernels for 0%

commit v1 on v0

v1 whole, which is shorter than its diff:
```python
import math

import jax
import jax.numpy as jnp
from jax import lax
from jax.sharding import Mesh, PartitionSpec as P

ROW = ("x", "y")
COL = ("z", "core")
SWAP = ((0, 1), (1, 0))
SIDE, DEPTH = 4, 16

EXCHANGE = ("x", "y", "core")


def place(x, y, core):
    return (x * SIDE + y) * 2 + core


ALONG_X = {c: [[place(i, j, c) for i in range(SIDE)] for j in range(SIDE)] for c in (0, 1)}
ALONG_Y = {c: [[place(j, i, c) for i in range(SIDE)] for j in range(SIDE)] for c in (0, 1)}
FIRST = ALONG_X[0] + ALONG_Y[1]
SECOND = ALONG_Y[0] + ALONG_X[1]


def exchange(value, groups):
    return lax.all_to_all(value, EXCHANGE, 0, 0, axis_index_groups=groups)


def spread(value, groups):
    return exchange(jnp.broadcast_to(value, (SIDE,) + value.shape), groups)


def gelu_parts(hidden):
    coeff = math.sqrt(2.0 / math.pi)
    inner = coeff * (hidden + 0.044715 * hidden * hidden * hidden)
    tangent = jnp.tanh(inner)
    active = 0.5 * hidden * (1.0 + tangent)
    slope = 0.5 * (1.0 + tangent) + 0.5 * hidden * (1.0 - tangent * tangent) * coeff * (
        1.0 + 3.0 * 0.044715 * hidden * hidden
    )
    return (active, slope)


def dot(left, right, left_dim, right_dim):
    return lax.dot_general(
        left,
        right,
        (((left_dim,), (right_dim,)), ((), ())),
        preferred_element_type=jnp.float32,
        precision=lax.Precision.HIGH,
    )


def on_device(tokens, w_in, w_out, out_grad):
    few, width = tokens.shape
    hid = w_in.shape[1]
    half = few * DEPTH
    total = 2 * half
    part = total // (SIDE * SIDE)

    both = jnp.concatenate([tokens, out_grad], axis=1)
    both = lax.all_gather(both, "z", axis=0, tiled=True)
    both = jnp.concatenate([both, lax.ppermute(both, "core", SWAP)], axis=0)
    tok, cot = both[:, :width], both[:, width:]

    hidden_p = dot(tok, w_in, 1, 0).reshape(SIDE, SIDE * part, hid)
    agrad_p = dot(cot, w_out, 1, 1).reshape(SIDE, SIDE * part, hid)
    sums = exchange(jnp.stack([hidden_p, agrad_p], axis=1), FIRST).sum(axis=0)
    sums = sums.reshape(2, SIDE, part, hid).transpose(1, 0, 2, 3)
    sums = exchange(sums, SECOND).sum(axis=0)

    active, slope = gelu_parts(sums[0])
    hgrad = sums[1] * slope

    full = spread(spread(jnp.stack([active, hgrad]), SECOND), FIRST)
    act = full[:, :, 0].reshape(total, hid)
    hg = full[:, :, 1].reshape(total, hid)

    res = jnp.concatenate([dot(act, w_out, 1, 0), dot(hg, w_in, 1, 1)], axis=1)
    res = res[:half] + lax.ppermute(res[half:], "core", SWAP)
    res = lax.all_to_all(res.reshape(DEPTH, few, 2 * width), "z", 0, 0).sum(axis=0)

    grad_out = dot(act, cot, 0, 0)
    grad_in = dot(tok, hg, 0, 0)
    return (res[:, :width], res[:, width:], grad_in, grad_out)


def solution(mesh):
    grid = Mesh(mesh.devices.reshape(SIDE, SIDE, DEPTH, 2), ("x", "y", "z", "core"))
    placed = (P(COL, ROW), P(ROW, COL), P(COL, ROW), P(COL, ROW))
    return jax.shard_map(
        on_device,
        mesh=grid,
        in_specs=placed,
        out_specs=(P(COL, ROW), P(COL, ROW), P(ROW, COL), P(COL, ROW)),
        check_vma=False,
    )
```

time: 577 us -> 173 us (0.30)
  the two profiles are of different devices: /device:TPU:22 before, /device:TPU:32 now
where the time goes in v1:
time: 173 us; the launch traced here: 172 us
  blocking collectives  106 us (61%)
  waiting for transfers between devices  33.1 us (19%)
  starting transfers between devices  12.8 us (7%)
  matrix products  10.1 us (6%)
  local copies, waits for them, and re-layouts  4.75 us (3%)
  other arithmetic  4.35 us (3%)
    all_to_all x4, blocking collectives, exchange(): return lax.all_to_all(value, EXCHANGE, 0, 0, axis_index_groups=groups)  69.5 us
    all_gather x1, blocking collectives, on_device(): both = lax.all_gather(both, 'z', axis=0, tiled=True)  36.8 us
    all_to_all x1, waiting for transfers between devices, on_device(): lax.all_to_all(res.reshape(DEPTH, few, 2 * width), 'z', 0, 0).sum(axis=0)  29 us
    dot_general x6, matrix products, dot(): lax.dot_general(left, right, (((left_dim,), (right_dim,)), ((), ())), pre...  10.1 us
    all_to_all x1, starting transfers between devices, on_device(): lax.all_to_all(res.reshape(DEPTH, few, 2 * width), 'z', 0, 0).sum(axis=0)  8.85 us
  transfers between devices with their start and end apart: 3, of which 3 were waited for; matrix products, arithmetic and copies ran while one was open for 3% of the time, Pallas kernels for 0%

profile of v1, /device:TPU:32, one launch (start us, length us, event | category | flops | bytes accessed | tf_op | source)
XLA Modules:
  0.0 172.1 jit_solution(10738122066017127943)
XLA Ops:
  0.6 0.9 pad_maximum_fusion.3
  1.6 36.8 %all_gather.3 = f32[256,640]{1,0:T(8,128)S(1)} all-gather(f32[16,640]{1,0:T(8,128)S(1)} %pad_maximum_fusion.3), channel_id=1, replica_groups=mesh['x'=4,'y'=4,'z'=16,'core'=2] {'z'}, dimensions={0}, use_global_device_ids=true | all-gather | bytes 696320 | tf_op jit(solution)/shard_map/all_gather | solution.py:63
  38.3 2.0 %collective-permute-start = (f32[256,640]{1,0:T(8,128)S(1)}, f32[256,640]{1,0:T(8,128)S(1)}, u32[]{:S(2)}, u32[]{:S(2)}) collective-permute-start(f32[256,640]{1,0:T(8,128)S(1)} %all_gather.3), channel_id=1, source_target_pairs={{0,1},{1,0},{2,3},{3,2},{4,5},{5,4},{6,7},{7,6},{8,9},{9,8},{10,11... | collective-permute-start | bytes 1966088 | tf_op jit(solution)/shard_map/ppermute | solution.py:64
  40.4 2.0 %collective-permute-done = f32[256,640]{1,0:T(8,128)S(1)} collective-permute-done((f32[256,640]{1,0:T(8,128)S(1)}, f32[256,640]{1,0:T(8,128)S(1)}, u32[]{:S(2)}, u32[]{:S(2)}) %collective-permute-start) | collective-permute-done | bytes 655392 | tf_op jit(solution)/shard_map/ppermute | solution.py:64
  42.5 1.4 fusion.2
  43.9 1.3 fusion.6
  45.4 23.4 %all_to_all.25 = f32[4,2,128,640]{3,2,1,0:T(8,128)S(1)} all-to-all(f32[4,2,128,640]{3,2,1,0:T(8,128)S(1)} %pad_maximum_fusion), channel_id=1, replica_groups={{0,128,256,384},{32,160,288,416},{64,192,320,448},{96,224,352,480},{1,3..., dimensions={0} | all-to-all | bytes 5242880 | tf_op jit(solution)/shard_map/all_to_all | solution.py:27
  68.8 1.0 reduce_sum.27
  69.9 1.1 copy.14
  71.0 13.0 %all_to_all.26 = f32[4,2,32,640]{3,2,1,0:T(8,128)S(1)} all-to-all(f32[4,2,32,640]{3,2,1,0:T(8,128)S(1)} %copy.14), channel_id=1, replica_groups={{0,32,64,96},{128,160,192,224},{256,288,320,352},{384,416,448,480},{1,1..., dimensions={0} | all-to-all | bytes 1310720 | tf_op jit(solution)/shard_map/all_to_all | solution.py:27
  84.2 11.2 %all_to_all.27 = f32[4,2,32,640]{3,2,1,0:T(8,128)S(1)} all-to-all(f32[4,2,32,640]{3,2,1,0:T(8,128)S(1)} %broadcast_in_dim.6), channel_id=1, replica_groups={{0,32,64,96},{128,160,192,224},{256,288,320,352},{384,416,448,480},{1,1..., dimensions={0} | all-to-all | bytes 1310720 | tf_op jit(solution)/shard_map/all_to_all | solution.py:27
  95.7 21.8 %all_to_all.28 = f32[4,4,2,32,640]{4,3,2,1,0:T(8,128)S(1)} all-to-all(f32[4,4,2,32,640]{4,3,2,1,0:T(8,128)S(1)} %broadcast_in_dim.7), channel_id=1, replica_groups={{0,128,256,384},{32,160,288,416},{64,192,320,448},{96,224,352,480},{1,3..., dimensions={0} | all-to-all | bytes 5242880 | tf_op jit(solution)/shard_map/all_to_all | solution.py:27
  117.7 1.0 fusion.19
  118.8 1.0 fusion.18
  119.9 1.9 %collective-permute-start.1 = (f32[256,640]{0,1:T(8,128)S(1)}, f32[256,640]{0,1:T(8,128)S(1)}, u32[]{:S(2)}, u32[]{:S(2)}) collective-permute-start(f32[256,640]{0,1:T(8,128)S(1)} %pad_maximum_fusion.1), channel_id=1, source_target_pairs={{0,1},{1,0},{2,3},{3,2},{4,5},{5,4},{6,7},{7,6},{8,9},{9,8},{10,11... | collective-permute-start | bytes 1966088 | tf_op jit(solution)/shard_map/ppermute | solution.py:81
  121.8 2.1 %collective-permute-done.1 = f32[256,640]{0,1:T(8,128)S(1)} collective-permute-done((f32[256,640]{0,1:T(8,128)S(1)}, f32[256,640]{0,1:T(8,128)S(1)}, u32[]{:S(2)}, u32[]{:S(2)}) %collective-permute-start.1) | collective-permute-done | bytes 655392 | tf_op jit(solution)/shard_map/ppermute | solution.py:81
  123.9 0.9 fusion.9
  124.8 2.2 %copy.15 = f32[256,640]{1,0:T(8,128)} copy(f32[256,640]{0,1:T(8,128)} %fusion.9) | data formatting | bytes 1310720 | tf_op jit(solution)/shard_map/add | solution.py:81
  127.0 8.8 %all-to-all-start.4 = ((f32[16,16,640]{2,1,0:T(8,128)}), f32[16,16,640]{2,1,0:T(8,128)}, u32[]{:S(2)}, u32[]{:S(2)}) async-start(f32[16,16,640]{2,1,0:T(8,128)} %bitcast.26), calls=%async_computation.4 | async-start | bytes 1310720 | tf_op jit(solution)/shard_map/all_to_all | solution.py:82
  135.8 3.2 %fusion.4 = f32[320,640]{1,0:T(8,128)} fusion(f32[512,640]{1,0:T(8,128)S(1)} %bitcast.23, f32[512,640]{1,0:T(8,128)} %copy-done.1), kind=kOutput, calls=%fused_computation.7 | convolution fusion | flops 629145600 | bytes 2916352 | tf_op jit(solution)/shard_map/dot_general | solution.py:46
  139.1 2.2 %fusion = f32[640,320]{0,1:T(8,128)} fusion(f32[512,640]{1,0:T(8,128)S(1)} %bitcast.21, f32[512,640]{1,0:T(8,128)S(1)} %copy-done.2), kind=kOutput, calls=%fused_computation.3 | convolution fusion | flops 629145600 | bytes 2916352 | tf_op jit(solution)/shard_map/dot_general | solution.py:46
  141.3 29.0 %all-to-all-done.4 = f32[16,16,640]{2,1,0:T(8,128)} async-done(((f32[16,16,640]{2,1,0:T(8,128)}), f32[16,16,640]{2,1,0:T(8,128)}, u32[]{:S(2)}, u32[]{:S(2)}) %all-to-all-start.4) | async-done | bytes 655392 | tf_op jit(solution)/shard_map/all_to_all | solution.py:82
  170.3 1.1 reduce_sum.29
  171.5 0.7 fusion.17
  (20 shorter events, 1.1 us)
Async XLA Ops:
  0.6 43.3 %copy-start = (f32[320,640]{1,0:T(8,128)S(1)}, f32[320,640]{1,0:T(8,128)}, u32[]{:S(2)}) copy-start(f32[320,640]{1,0:T(8,128)} %param.5) | copy-start | bytes 2457604
  38.3 4.2 %copy-start.3 = (f32[640,320]{0,1:T(8,128)S(1)}, f32[640,320]{0,1:T(8,128)}, u32[]{:S(2)}) copy-start(f32[640,320]{0,1:T(8,128)} %param.6) | copy-start | bytes 2457604
  38.3 4.1 %collective-permute-start = (f32[256,640]{1,0:T(8,128)S(1)}, f32[256,640]{1,0:T(8,128)S(1)}, u32[]{:S(2)}, u32[]{:S(2)}) collective-permute-start(f32[256,640]{1,0:T(8,128)S(1)} %all_gather.3), channel_id=1, source_target_pairs={{0,1},{1,0},{2,3},{3,2},{4,5},{5,4},{6,7},{7,6},{8,9},{9,8},{10,11... | collective-permute-start | bytes 1966088 | tf_op jit(solution)/shard_map/ppermute | solution.py:64
  42.5 1.4 copy-start.1
  117.7 1.1 copy-start.4
  119.9 4.0 %collective-permute-start.1 = (f32[256,640]{0,1:T(8,128)S(1)}, f32[256,640]{0,1:T(8,128)S(1)}, u32[]{:S(2)}, u32[]{:S(2)}) collective-permute-start(f32[256,640]{0,1:T(8,128)S(1)} %pad_maximum_fusion.1), channel_id=1, source_target_pairs={{0,1},{1,0},{2,3},{3,2},{4,5},{5,4},{6,7},{7,6},{8,9},{9,8},{10,11... | collective-permute-start | bytes 1966088 | tf_op jit(solution)/shard_map/ppermute | solution.py:81
  127.0 43.3 %all-to-all-start.4 = ((f32[16,16,640]{2,1,0:T(8,128)}), f32[16,16,640]{2,1,0:T(8,128)}, u32[]{:S(2)}, u32[]{:S(2)}) async-start(f32[16,16,640]{2,1,0:T(8,128)} %bitcast.26), calls=%async_computation.4 | async-start | bytes 1310720 | tf_op jit(solution)/shard_map/all_to_all | solution.py:82
  135.8 3.2 %copy-start.2 = (f32[512,640]{1,0:T(8,128)S(1)}, f32[512,640]{1,0:T(8,128)}, u32[]{:S(2)}) copy-start(f32[512,640]{1,0:T(8,128)} %copy-done.1) | copy-start | bytes 3932164

commit v2 on v1

v2 whole, which is shorter than its diff:
```python
import math

import jax
import jax.numpy as jnp
from jax import lax
from jax.experimental import pallas as pl
from jax.experimental.pallas import tpu as pltpu
from jax.sharding import Mesh, PartitionSpec as P

ROW = ("x", "y")
COL = ("z", "core")
SWAP = ((0, 1), (1, 0))
SIDE, DEPTH = 4, 16
ROWS = SIDE * SIDE

def gelu_parts(hidden):
    coeff = math.sqrt(2.0 / math.pi)
    inner = coeff * (hidden + 0.044715 * hidden * hidden * hidden)
    tangent = jnp.tanh(inner)
    active = 0.5 * hidden * (1.0 + tangent)
    slope = 0.5 * (1.0 + tangent) + 0.5 * hidden * (1.0 - tangent * tangent) * coeff * (
        1.0 + 3.0 * 0.044715 * hidden * hidden
    )
    return (active, slope)


def dot(left, right, left_dim, right_dim):
    return lax.dot_general(
        left,
        right,
        (((left_dim,), (right_dim,)), ((), ())),
        preferred_element_type=jnp.float32,
        precision=lax.Precision.HIGH,
    )


def halves(value):
    high = value.astype(jnp.bfloat16)
    return high, (value - high.astype(jnp.float32)).astype(jnp.bfloat16)


def dot3(left, right, dims):
    def one(a, b):
        return lax.dot_general(a, b, (dims, ((), ())), preferred_element_type=jnp.float32)

    return one(left[0], right[0]) + one(left[0], right[1]) + one(left[1], right[0])


def whole(value):
    return (value,)


def dot_f32(left, right, dims):
    return lax.dot_general(
        left[0], right[0], (dims, ((), ())), precision=lax.Precision.HIGHEST, preferred_element_type=jnp.float32
    )


def local_call(body, out_shape, *operands):
    return pl.pallas_call(
        body,
        out_shape=out_shape,
        in_specs=[pl.BlockSpec(memory_space=pltpu.VMEM)] * len(operands),
        out_specs=jax.tree.map(lambda _: pl.BlockSpec(memory_space=pltpu.VMEM), out_shape),
        compiler_params=pltpu.CompilerParams(vmem_limit_bytes=40 * 2**20),
    )(*operands)


def first_products(pieces, dot, both_ref, w_in_ref, w_out_ref, other_ref, sums_ref):
    width, hid = w_in_ref.shape
    wide = 384
    spare = jnp.zeros((wide - width, hid), jnp.float32)
    tok = pieces(both_ref[:, :wide])
    cot = pieces(both_ref[:, 2 * width - wide :])
    shape = sums_ref.shape[:1] + sums_ref.shape[3:]
    for block, (w_in, w_out) in enumerate(((w_in_ref[...], w_out_ref[...]), (other_ref[0], other_ref[1]))):
        w_in = pieces(jnp.concatenate([w_in, spare], axis=0))
        w_out = pieces(jnp.concatenate([spare, w_out], axis=0))
        sums_ref[:, 0, block] = dot(tok, w_in, ((1,), (0,))).reshape(shape)
        sums_ref[:, 1, block] = dot(cot, w_out, ((1,), (0,))).reshape(shape)


def first_body(*refs):
    core = lax.axis_index("core")

    @pl.when(core == 0)
    def _():
        first_products(whole, dot_f32, *refs)

    @pl.when(core == 1)
    def _():
        first_products(halves, dot3, *refs)


def middle_body(parts_ref, mine_ref):
    sums = parts_ref[0]
    for i in range(1, ROWS):
        sums = sums + parts_ref[i]
    active, slope = gelu_parts(sums[0])
    hgrad = sums[1] * slope
    for i in range(ROWS):
        mine_ref[i, 0] = active
        mine_ref[i, 1] = hgrad


def second_body(full_ref, w_in_ref, w_out_ref, other_ref, res_ref):
    width, hid = w_in_ref.shape
    total = res_ref.shape[0]
    out = inn = None
    for block, (w_in, w_out) in enumerate(((w_in_ref[...], w_out_ref[...]), (other_ref[0], other_ref[1]))):
        act = halves(full_ref[:, 0, block].reshape(total, hid))
        hg = halves(full_ref[:, 1, block].reshape(total, hid))
        o = dot3(halves(w_out), act, ((1,), (1,)))
        i = dot3(halves(w_in), hg, ((1,), (1,)))
        out, inn = (o, i) if block == 0 else (out + o, inn + i)
    res_ref[...] = jnp.concatenate([out, inn], axis=0).T


def last_body(parts_ref, output_ref, in_grad_ref):
    width = output_ref.shape[1]
    total = parts_ref[0]
    for i in range(1, parts_ref.shape[0]):
        total = total + parts_ref[i]
    output_ref[...] = total[:, :width]
    in_grad_ref[...] = total[:, width:]


def floats(*shape):
    return jax.ShapeDtypeStruct(shape, jnp.float32)


def on_device(tokens, w_in, w_out, out_grad):
    few, width = tokens.shape
    hid = w_in.shape[1]
    total = few * DEPTH
    part = total // ROWS

    w_out = w_out.T
    other = lax.ppermute(jnp.stack([w_in, w_out]), "core", SWAP)

    both = lax.all_gather(jnp.concatenate([tokens, out_grad], axis=1), "z", axis=0, tiled=True)

    shape = floats(ROWS, 2, 2, part, hid)
    sums = local_call(first_body, shape, both, w_in, w_out, other)
    sums = lax.all_to_all(sums, ROW, 0, 0)

    full = lax.all_to_all(local_call(middle_body, shape, sums), ROW, 0, 0)

    res = local_call(second_body, floats(total, 2 * width), full, w_in, w_out, other)
    res = lax.all_to_all(res.reshape(DEPTH, few, 2 * width), "z", 0, 0)

    acts = [full[:, 0, i].reshape(total, hid) for i in (0, 1)]
    hgs = [full[:, 1, i].reshape(total, hid) for i in (0, 1)]
    tok, cot = both[:, :width], both[:, width:]
    grads_in = [dot(tok, h, 0, 0) for h in hgs]
    grads_out = [dot(cot, a, 0, 0) for a in acts]
    grad_in = grads_in[0] + lax.ppermute(grads_in[1], "core", SWAP)
    grad_out = grads_out[0] + lax.ppermute(grads_out[1], "core", SWAP)

    output, in_grad = local_call(last_body, (floats(few, width), floats(few, width)), res)
    return (output, in_grad, grad_in, grad_out.T)


def solution(mesh):
    grid = Mesh(mesh.devices.reshape(SIDE, SIDE, DEPTH, 2), ("x", "y", "z", "core"))
    placed = (P(COL, ROW), P(ROW, COL), P(COL, ROW), P(COL, ROW))
    return jax.shard_map(
        on_device,
        mesh=grid,
        in_specs=placed,
        out_specs=(P(COL, ROW), P(COL, ROW), P(ROW, COL), P(COL, ROW)),
        check_vma=False,
    )
```

time: 173 us -> 144 us (0.83)
  waiting for transfers between devices: 33.1 us -> 14.4 us
  blocking collectives: 106 us -> 96.9 us
  Pallas kernels: 0 us -> 8.72 us
  matrix products: 10.1 us -> 4.58 us
  local copies, waits for them, and re-layouts: 4.75 us -> 1.09 us
  other arithmetic: 4.35 us -> 1.69 us
  starting transfers between devices: 12.8 us -> 15.1 us
    all_to_all x1, waiting for transfers between devices: 29 us -> 14 us  [on_device(): res = lax.all_to_all(res.reshape(DEPTH, few, 2 * width), 'z', 0, 0)]
    all_to_all x4 -> x2, blocking collectives: 69.5 us -> 59.9 us  [the longest x1 32.1 us: on_device(): sums = lax.all_to_all(sums, ROW, 0, 0)]
    pallas_call x0 -> x4, Pallas kernels: none -> 8.72 us  [local_call(): pl.pallas_call(body, out_shape=out_shape, in_specs=[pl.BlockSpec(memory_s...]
    dot_general x6 -> x4, matrix products: 10.1 us -> 4.58 us  [dot(): lax.dot_general(left, right, (((left_dim,), (right_dim,)), ((), ())), pre...]
    ppermute x2 -> x3, waiting for transfers between devices: 4.07 us -> 0.39 us  [the longest x1 0.39 us: on_device(): grad_out = grads_out[0] + lax.ppermute(grads_out[1], 'core', SWAP)]
    ppermute x2 -> x3, starting transfers between devices: 3.96 us -> 6.25 us  [the longest x1 2.41 us: on_device(): grad_out = grads_out[0] + lax.ppermute(grads_out[1], 'core', SWAP)]
    reduce_sum x3 -> x0, other arithmetic: 2.19 us -> none  [the longest x1 1.13 us: on_device(): lax.all_to_all(res.reshape(DEPTH, few, 2 * width), 'z', 0, 0).sum(axis=0)]
    add x1 -> x0, local copies, waits for them, and re-layouts: 2.16 us -> none  [on_device(): res = res[:half] + lax.ppermute(res[half:], 'core', SWAP)]
  transfers between devices with their start and end apart: 3 -> 4, of which waited for: 3 -> 2; matrix products, arithmetic and copies ran while one was open for 3% -> 3% of each run, Pallas kernels for 0% -> 0%
where the time goes in v2:
time: 144 us; the launch traced here: 143 us
  blocking collectives  96.9 us (67%)
  starting transfers between devices  15.1 us (10%)
  waiting for transfers between devices  14.4 us (10%)
  Pallas kernels  8.72 us (6%)
  matrix products  4.58 us (3%)
  other arithmetic  1.69 us (1%)
    all_gather x1, blocking collectives, on_device(): lax.all_gather(jnp.concatenate([tokens, out_grad], axis=1), 'z', axis=0,...  36.9 us
    all_to_all x1, blocking collectives, on_device(): sums = lax.all_to_all(sums, ROW, 0, 0)  32.1 us
    all_to_all x1, blocking collectives, on_device(): full = lax.all_to_all(local_call(middle_body, shape, sums), ROW, 0, 0)  27.8 us
    all_to_all x1, waiting for transfers between devices, on_device(): res = lax.all_to_all(res.reshape(DEPTH, few, 2 * width), 'z', 0, 0)  14 us
    all_to_all x1, starting transfers between devices, on_device(): res = lax.all_to_all(res.reshape(DEPTH, few, 2 * width), 'z', 0, 0)  8.87 us
    pallas_call x4, Pallas kernels, local_call(): pl.pallas_call(body, out_shape=out_shape, in_specs=[pl.BlockSpec(memory_s...  8.72 us
    dot_general x4, matrix products, dot(): lax.dot_general(left, right, (((left_dim,), (right_dim,)), ((), ())), pre...  4.58 us
  transfers between devices with their start and end apart: 4, of which 2 were waited for; matrix products, arithmetic and copies ran while one was open for 3% of the time, Pallas kernels for 0%

profile of v2, /device:TPU:32, one launch (start us, length us, event | category | flops | bytes accessed | tf_op | source)
XLA Modules:
  0.0 143.3 jit_solution(15069618084221329810)
XLA Ops:
  0.7 1.6 %pad_maximum_fusion = f32[2,320,640]{2,1,0:T(8,128)S(1)} fusion(f32[1,320,640]{2,1,0:T(8,128)} %bitcast.16, f32[1,320,640]{2,1,0:T(8,128)} %bitcast.15), kind=kLoop, calls=%fused_computation | loop fusion | flops 409600 | bytes 3276800 | tf_op jit(solution)/shard_map/stack | solution.py:139
  2.3 1.9 %collective-permute-start = (f32[2,320,640]{2,1,0:T(8,128)S(1)}, f32[2,320,640]{2,1,0:T(8,128)S(1)}, u32[]{:S(2)}, u32[]{:S(2)}) collective-permute-start(f32[2,320,640]{2,1,0:T(8,128)S(1)} %pad_maximum_fusion), channel_id=1, source_target_pairs={{0,1},{1,0},{2,3},{3,2},{4,5},{5,4},{6,7},{7,6},{8,9},{9,8},{10,11... | collective-permute-start | bytes 4915208 | tf_op jit(solution)/shard_map/ppermute | solution.py:139
  4.2 0.1 pad_maximum_fusion.1
  4.3 36.9 %all_gather.3.refs_0_ = f32[256,640]{1,0:T(8,128)S(1)} all-gather(f32[16,640]{1,0:T(8,128)S(1)} %pad_maximum_fusion.1), channel_id=1, replica_groups=mesh['x'=4,'y'=4,'z'=16,'core'=2] {'z'}, dimensions={0}, use_global_device_ids=true | all-gather | bytes 696320 | tf_op jit(solution)/shard_map/all_gather | solution.py:141
  41.3 0.0 collective-permute-done.refs_3_.other_ref
  41.3 4.7 %shard_map.75 = f32[16,2,2,16,640]{4,3,2,1,0:T(8,128)S(1)} custom-call(f32[256,640]{1,0:T(8,128)S(1)} %all_gather.3.refs_0_, f32[320,640]{1,0:T(8,128)S(1)} %copy-done, f32[320,640]{1,0:T(8,128)S(1)} %bitcast.17, f32[2,320,640]{2,1,0:T(8,128)S(1)} %collective-permute-done.refs_3_.other_ref), custom_call_target="tpu_custom_call" | custom-call | tf_op jit(solution)/shard_map/pallas_call | solution.py:60
  46.0 32.1 %all_to_all.15.parts_ref = f32[16,2,2,16,640]{4,3,2,1,0:T(8,128)S(1)} all-to-all(f32[16,2,2,16,640]{4,3,2,1,0:T(8,128)S(1)} %shard_map.75), channel_id=1, replica_groups=mesh['x'=4,'y'=4,'z'=16,'core'=2] {'x','y'}, dimensions={0} | all-to-all | bytes 5242880 | tf_op jit(solution)/shard_map/all_to_all | solution.py:145
  78.2 0.3 shard_map.76
  78.5 27.8 %all_to_all.16.full_ref = f32[16,2,2,16,640]{4,3,2,1,0:T(8,128)S(1)} all-to-all(f32[16,2,2,16,640]{4,3,2,1,0:T(8,128)S(1)} %shard_map.76), channel_id=1, replica_groups=mesh['x'=4,'y'=4,'z'=16,'core'=2] {'x','y'}, dimensions={0} | all-to-all | bytes 5242880 | tf_op jit(solution)/shard_map/all_to_all | solution.py:147
  106.3 1.9 %shard_map.77 = f32[256,640]{1,0:T(8,128)S(1)} custom-call(f32[16,2,2,16,640]{4,3,2,1,0:T(8,128)S(1)} %all_to_all.16.full_ref, f32[320,640]{1,0:T(8,128)S(1)} %copy-done, f32[320,640]{1,0:T(8,128)S(1)} %bitcast.18, f32[2,320,640]{2,1,0:T(8,128)S(1)} %collective-permute-done.refs_3_.other_ref), custom_call_target="tpu_custom_call" | custom-call | tf_op jit(solution)/shard_map/pallas_call | solution.py:60
  108.2 0.0 copy-start.2
  108.2 0.8 copy-done.2
  109.0 8.9 %all-to-all-start.2 = ((f32[16,16,640]{2,1,0:T(8,128)}), f32[16,16,640]{2,1,0:T(8,128)}, u32[]{:S(2)}, u32[]{:S(2)}) async-start(f32[16,16,640]{2,1,0:T(8,128)} %bitcast.19), calls=%async_computation.2 | async-start | bytes 1310720 | tf_op jit(solution)/shard_map/all_to_all | solution.py:150
  117.9 0.2 fusion.7
  118.1 0.6 fusion.4
  118.8 1.9 %collective-permute-start.1 = (f32[320,640]{1,0:T(8,128)S(1)}, f32[320,640]{1,0:T(8,128)S(1)}, u32[]{:S(2)}, u32[]{:S(2)}) collective-permute-start(f32[320,640]{1,0:T(8,128)S(1)} %fusion.4), channel_id=1, source_target_pairs={{0,1},{1,0},{2,3},{3,2},{4,5},{5,4},{6,7},{7,6},{8,9},{9,8},{10,11... | collective-permute-start | bytes 2457608 | tf_op jit(solution)/shard_map/ppermute | solution.py:157
  120.7 0.8 fusion.1
  121.5 2.4 %collective-permute-start.2 = (f32[320,640]{1,0:T(8,128)S(1)}, f32[320,640]{1,0:T(8,128)S(1)}, u32[]{:S(2)}, u32[]{:S(2)}) collective-permute-start(f32[320,640]{1,0:T(8,128)S(1)} %fusion.1), channel_id=1, source_target_pairs={{0,1},{1,0},{2,3},{3,2},{4,5},{5,4},{6,7},{7,6},{8,9},{9,8},{10,11... | collective-permute-start | bytes 2457608 | tf_op jit(solution)/shard_map/ppermute | solution.py:158
  123.9 0.0 collective-permute-done.1
  123.9 1.5 %convolution_add_fusion.1 = f32[320,640]{1,0:T(8,128)} fusion(f32[320,640]{1,0:T(8,128)S(1)} %collective-permute-done.1, f32[256,640]{1,0:T(8,128)S(1)} %bitcast.23, f32[256,640]{1,0:T(8,128)S(1)} %all_gather.3.refs_0_), kind=kOutput, calls=%fused_computation.3 | convolution fusion | flops 314777600 | bytes 2686976 | tf_op jit(solution)/shard_map/dot_general | solution.py:28
  125.4 0.4 collective-permute-done.2
  125.8 1.6 %fusion = f32[640,320]{0,1:T(8,128)} fusion(f32[320,640]{1,0:T(8,128)S(1)} %collective-permute-done.2, f32[256,640]{1,0:T(8,128)S(1)} %bitcast.22, f32[256,640]{1,0:T(8,128)S(1)} %all_gather.3.refs_0_), kind=kOutput, calls=%fused_computation.2 | convolution fusion | flops 314777600 | bytes 2686976 | tf_op jit(solution)/shard_map/dot_general | solution.py:28
  127.5 14.0 %all-to-all-done.2.parts_ref = f32[16,16,640]{2,1,0:T(8,128)} async-done(((f32[16,16,640]{2,1,0:T(8,128)}), f32[16,16,640]{2,1,0:T(8,128)}, u32[]{:S(2)}, u32[]{:S(2)}) %all-to-all-start.2) | async-done | bytes 655392 | tf_op jit(solution)/shard_map/all_to_all | solution.py:150
  141.5 1.8 %shard_map.78 = (f32[16,320]{1,0:T(8,128)}, f32[16,320]{1,0:T(8,128)}) custom-call(f32[16,16,640]{2,1,0:T(8,128)} %all-to-all-done.2.parts_ref), custom_call_target="tpu_custom_call" | custom-call | tf_op jit(solution)/shard_map/pallas_call | solution.py:60
  (8 shorter events, 0.0 us)
Async XLA Ops:
  0.6 40.6 %copy-start.1 = (f32[640,320]{0,1:T(8,128)S(1)}, f32[640,320]{0,1:T(8,128)}, u32[]{:S(2)}) copy-start(f32[640,320]{0,1:T(8,128)} %param.6) | copy-start | bytes 2457604
  0.6 40.6 %copy-start = (f32[320,640]{1,0:T(8,128)S(1)}, f32[320,640]{1,0:T(8,128)}, u32[]{:S(2)}) copy-start(f32[320,640]{1,0:T(8,128)} %w_in_ref.1) | copy-start | bytes 2457604
  0.7 3.6 %copy-start.3 = (f32[16,320]{1,0:T(8,128)S(1)}, f32[16,320]{1,0:T(8,128)}, u32[]{:S(2)}) copy-start(f32[16,320]{1,0:T(8,128)} %param.7) | copy-start | bytes 61444
  0.7 3.6 %copy-start.4 = (f32[16,320]{1,0:T(8,128)S(1)}, f32[16,320]{1,0:T(8,128)}, u32[]{:S(2)}) copy-start(f32[16,320]{1,0:T(8,128)} %param.4) | copy-start | bytes 61444
  2.3 39.0 %collective-permute-start = (f32[2,320,640]{2,1,0:T(8,128)S(1)}, f32[2,320,640]{2,1,0:T(8,128)S(1)}, u32[]{:S(2)}, u32[]{:S(2)}) collective-permute-start(f32[2,320,640]{2,1,0:T(8,128)S(1)} %pad_maximum_fusion), channel_id=1, source_target_pairs={{0,1},{1,0},{2,3},{3,2},{4,5},{5,4},{6,7},{7,6},{8,9},{9,8},{10,11... | collective-permute-start | bytes 4915208 | tf_op jit(solution)/shard_map/ppermute | solution.py:139
  108.2 0.8 copy-start.2
  109.0 32.5 %all-to-all-start.2 = ((f32[16,16,640]{2,1,0:T(8,128)}), f32[16,16,640]{2,1,0:T(8,128)}, u32[]{:S(2)}, u32[]{:S(2)}) async-start(f32[16,16,640]{2,1,0:T(8,128)} %bitcast.19), calls=%async_computation.2 | async-start | bytes 1310720 | tf_op jit(solution)/shard_map/all_to_all | solution.py:150
  118.8 5.1 %collective-permute-start.1 = (f32[320,640]{1,0:T(8,128)S(1)}, f32[320,640]{1,0:T(8,128)S(1)}, u32[]{:S(2)}, u32[]{:S(2)}) collective-permute-start(f32[320,640]{1,0:T(8,128)S(1)} %fusion.4), channel_id=1, source_target_pairs={{0,1},{1,0},{2,3},{3,2},{4,5},{5,4},{6,7},{7,6},{8,9},{9,8},{10,11... | collective-permute-start | bytes 2457608 | tf_op jit(solution)/shard_map/ppermute | solution.py:157
  121.5 4.4 %collective-permute-start.2 = (f32[320,640]{1,0:T(8,128)S(1)}, f32[320,640]{1,0:T(8,128)S(1)}, u32[]{:S(2)}, u32[]{:S(2)}) collective-permute-start(f32[320,640]{1,0:T(8,128)S(1)} %fusion.1), channel_id=1, source_target_pairs={{0,1},{1,0},{2,3},{3,2},{4,5},{5,4},{6,7},{7,6},{8,9},{9,8},{10,11... | collective-permute-start | bytes 2457608 | tf_op jit(solution)/shard_map/ppermute | solution.py:158

commit v3 on v2

--- a/solution.py
+++ b/solution.py
@@ -39,21 +39,27 @@
     return high, (value - high.astype(jnp.float32)).astype(jnp.bfloat16)
 
 
-def dot3(left, right, dims):
-    def one(a, b):
-        return lax.dot_general(a, b, (dims, ((), ())), preferred_element_type=jnp.float32)
-
-    return one(left[0], right[0]) + one(left[0], right[1]) + one(left[1], right[0])
+def stacked(value, order, axis):
+    parts = halves(value)
+    return jnp.concatenate([parts[i] for i in order], axis=axis)
 
 
-def whole(value):
-    return (value,)
+def exact_dot(left, right):
+    def thirds(value):
+        high, _ = halves(value)
+        return (high,) + halves(value - high.astype(jnp.float32))
+
+    left, right = thirds(left), thirds(right)
+    total = None
+    for order in (4, 3, 2, 1, 0):
+        for i in range(3):
+            if 0 <= order - i < 3:
+                term = jnp.dot(left[i], right[order - i], preferred_element_type=jnp.float32)
+                total = term if total is None else total + term
+    return total
 
 
-def dot_f32(left, right, dims):
-    return lax.dot_general(
-        left[0], right[0], (dims, ((), ())), precision=lax.Precision.HIGHEST, preferred_element_type=jnp.float32
-    )
+LEFT, RIGHT = (0, 1, 0), (0, 0, 1)
 
 
 def local_call(body, out_shape, *operands):
@@ -66,30 +72,30 @@
     )(*operands)
 
 
-def first_products(pieces, dot, both_ref, w_in_ref, w_out_ref, other_ref, sums_ref):
+def first_body(both_ref, w_in_ref, w_out_ref, other_ref, sums_ref):
     width, hid = w_in_ref.shape
     wide = 384
-    spare = jnp.zeros((wide - width, hid), jnp.float32)
-    tok = pieces(both_ref[:, :wide])
-    cot = pieces(both_ref[:, 2 * width - wide :])
+    spare = jnp.zeros((wide - width, 2 * hid), jnp.float32)
     shape = sums_ref.shape[:1] + sums_ref.shape[3:]
-    for block, (w_in, w_out) in enumerate(((w_in_ref[...], w_out_ref[...]), (other_ref[0], other_ref[1]))):
-        w_in = pieces(jnp.concatenate([w_in, spare], axis=0))
-        w_out = pieces(jnp.concatenate([spare, w_out], axis=0))
-        sums_ref[:, 0, block] = dot(tok, w_in, ((1,), (0,))).reshape(shape)
-        sums_ref[:, 1, block] = dot(cot, w_out, ((1,), (0,))).reshape(shape)
+    core = lax.axis_index("core")
 
+    def weights(which):
+        return jnp.concatenate([(w_in_ref, w_out_ref)[which][...], other_ref[which]], axis=1)
 
-def first_body(*refs):
-    core = lax.axis_index("core")
+    def products(dot):
+        tok = dot(both_ref[:, :wide], jnp.concatenate([weights(0), spare], axis=0))
+        cot = dot(both_ref[:, 2 * width - wide :], jnp.concatenate([spare, weights(1)], axis=0))
+        for which, result in enumerate((tok, cot)):
+            for block in (0, 1):
+                sums_ref[:, which, block] = result[:, block * hid : (block + 1) * hid].reshape(shape)
 
     @pl.when(core == 0)
     def _():
-        first_products(whole, dot_f32, *refs)
+        products(exact_dot)
 
     @pl.when(core == 1)
     def _():
-        first_products(halves, dot3, *refs)
+        products(lambda a, b: jnp.dot(stacked(a, LEFT, 1), stacked(b, RIGHT, 0), preferred_element_type=jnp.float32))
 
 
 def middle_body(parts_ref, mine_ref):
@@ -104,16 +110,20 @@
 
 
 def second_body(full_ref, w_in_ref, w_out_ref, other_ref, res_ref):
-    width, hid = w_in_ref.shape
     total = res_ref.shape[0]
-    out = inn = None
-    for block, (w_in, w_out) in enumerate(((w_in_ref[...], w_out_ref[...]), (other_ref[0], other_ref[1]))):
-        act = halves(full_ref[:, 0, block].reshape(total, hid))
-        hg = halves(full_ref[:, 1, block].reshape(total, hid))
-        o = dot3(halves(w_out), act, ((1,), (1,)))
-        i = dot3(halves(w_in), hg, ((1,), (1,)))
-        out, inn = (o, i) if block == 0 else (out + o, inn + i)
-    res_ref[...] = jnp.concatenate([out, inn], axis=0).T
+    hid = w_in_ref.shape[1]
+
+    def product(which, w_ref):
+        weights = jnp.concatenate([w_ref[...], other_ref[1 - which]], axis=1)
+        rows = jnp.concatenate([full_ref[:, which, i].reshape(total, hid) for i in (0, 1)], axis=1)
+        return lax.dot_general(
+            stacked(weights, LEFT, 1),
+            stacked(rows, RIGHT, 1),
+            (((1,), (1,)), ((), ())),
+            preferred_element_type=jnp.float32,
+        )
+
+    res_ref[...] = jnp.concatenate([product(0, w_out_ref), product(1, w_in_ref)], axis=0).T
 
 
 def last_body(parts_ref, output_ref, in_grad_ref):

time: 144 us -> 141 us (0.979)
  waiting for transfers between devices: 14.4 us -> 12.1 us
  blocking collectives: 96.9 us -> 94.9 us
    all_to_all x1, waiting for transfers between devices: 14 us -> 11.7 us  [on_device(): res = lax.all_to_all(res.reshape(DEPTH, few, 2 * width), 'z', 0, 0)]
    all_to_all x1, blocking collectives: 27.8 us -> 26.2 us  [on_device(): full = lax.all_to_all(local_call(middle_body, shape, sums), ROW, 0, 0)]
where the time goes in v3:
time: 141 us; the launch traced here: 140 us
  blocking collectives  94.9 us (67%)
  starting transfers between devices  15.1 us (11%)
  waiting for transfers between devices  12.1 us (9%)
  Pallas kernels  10.1 us (7%)
  matrix products  4.58 us (3%)
  other arithmetic  1.69 us (1%)
    all_gather x1, blocking collectives, on_device(): lax.all_gather(jnp.concatenate([tokens, out_grad], axis=1), 'z', axis=0,...  36.9 us
    all_to_all x1, blocking collectives, on_device(): sums = lax.all_to_all(sums, ROW, 0, 0)  31.7 us
    all_to_all x1, blocking collectives, on_device(): full = lax.all_to_all(local_call(middle_body, shape, sums), ROW, 0, 0)  26.2 us
    all_to_all x1, waiting for transfers between devices, on_device(): res = lax.all_to_all(res.reshape(DEPTH, few, 2 * width), 'z', 0, 0)  11.7 us
    pallas_call x4, Pallas kernels, local_call(): pl.pallas_call(body, out_shape=out_shape, in_specs=[pl.BlockSpec(memory_s...  10.1 us
    all_to_all x1, starting transfers between devices, on_device(): res = lax.all_to_all(res.reshape(DEPTH, few, 2 * width), 'z', 0, 0)  8.87 us
    dot_general x4, matrix products, dot(): lax.dot_general(left, right, (((left_dim,), (right_dim,)), ((), ())), pre...  4.58 us
  transfers between devices with their start and end apart: 4, of which 2 were waited for; matrix products, arithmetic and copies ran while one was open for 3% of the time, Pallas kernels for 0%

profile of v3, /device:TPU:32, one launch (start us, length us, event | category | flops | bytes accessed | tf_op | source)
XLA Modules:
  0.0 140.3 jit_solution(7372473697850465809)
XLA Ops:
  0.6 0.0 copy-start.1
  0.7 1.6 %pad_maximum_fusion = f32[2,320,640]{2,1,0:T(8,128)S(1)} fusion(f32[1,320,640]{2,1,0:T(8,128)} %bitcast.16, f32[1,320,640]{2,1,0:T(8,128)} %bitcast.15), kind=kLoop, calls=%fused_computation | loop fusion | flops 409600 | bytes 3276800 | tf_op jit(solution)/shard_map/stack | solution.py:149
  2.3 1.9 %collective-permute-start = (f32[2,320,640]{2,1,0:T(8,128)S(1)}, f32[2,320,640]{2,1,0:T(8,128)S(1)}, u32[]{:S(2)}, u32[]{:S(2)}) collective-permute-start(f32[2,320,640]{2,1,0:T(8,128)S(1)} %pad_maximum_fusion), channel_id=1, source_target_pairs={{0,1},{1,0},{2,3},{3,2},{4,5},{5,4},{6,7},{7,6},{8,9},{9,8},{10,11... | collective-permute-start | bytes 4915208 | tf_op jit(solution)/shard_map/ppermute | solution.py:149
  4.2 0.1 pad_maximum_fusion.1
  4.3 36.9 %all_gather.3.both_ref = f32[256,640]{1,0:T(8,128)S(1)} all-gather(f32[16,640]{1,0:T(8,128)S(1)} %pad_maximum_fusion.1), channel_id=1, replica_groups=mesh['x'=4,'y'=4,'z'=16,'core'=2] {'z'}, dimensions={0}, use_global_device_ids=true | all-gather | bytes 696320 | tf_op jit(solution)/shard_map/all_gather | solution.py:151
  41.3 0.0 collective-permute-done.other_ref
  41.3 6.4 %shard_map.75 = f32[16,2,2,16,640]{4,3,2,1,0:T(8,128)S(1)} custom-call(f32[256,640]{1,0:T(8,128)S(1)} %all_gather.3.both_ref, f32[320,640]{1,0:T(8,128)S(1)} %copy-done, f32[320,640]{1,0:T(8,128)S(1)} %bitcast.17, f32[2,320,640]{2,1,0:T(8,128)S(1)} %collective-permute-done.other_ref), custom_call_target="tpu_custom_call" | custom-call | tf_op jit(solution)/shard_map/pallas_call | solution.py:66
  47.7 31.7 %all_to_all.15.parts_ref = f32[16,2,2,16,640]{4,3,2,1,0:T(8,128)S(1)} all-to-all(f32[16,2,2,16,640]{4,3,2,1,0:T(8,128)S(1)} %shard_map.75), channel_id=1, replica_groups=mesh['x'=4,'y'=4,'z'=16,'core'=2] {'x','y'}, dimensions={0} | all-to-all | bytes 5242880 | tf_op jit(solution)/shard_map/all_to_all | solution.py:155
  79.4 0.3 shard_map.76
  79.7 26.2 %all_to_all.16.full_ref = f32[16,2,2,16,640]{4,3,2,1,0:T(8,128)S(1)} all-to-all(f32[16,2,2,16,640]{4,3,2,1,0:T(8,128)S(1)} %shard_map.76), channel_id=1, replica_groups=mesh['x'=4,'y'=4,'z'=16,'core'=2] {'x','y'}, dimensions={0} | all-to-all | bytes 5242880 | tf_op jit(solution)/shard_map/all_to_all | solution.py:157
  105.9 1.6 %shard_map.77 = f32[256,640]{1,0:T(8,128)S(1)} custom-call(f32[16,2,2,16,640]{4,3,2,1,0:T(8,128)S(1)} %all_to_all.16.full_ref, f32[320,640]{1,0:T(8,128)S(1)} %copy-done, f32[320,640]{1,0:T(8,128)S(1)} %bitcast.18, f32[2,320,640]{2,1,0:T(8,128)S(1)} %collective-permute-done.other_ref), custom_call_target="tpu_custom_call" | custom-call | tf_op jit(solution)/shard_map/pallas_call | solution.py:66
  107.6 0.8 copy-done.2
  108.4 8.9 %all-to-all-start.2 = ((f32[16,16,640]{2,1,0:T(8,128)}), f32[16,16,640]{2,1,0:T(8,128)}, u32[]{:S(2)}, u32[]{:S(2)}) async-start(f32[16,16,640]{2,1,0:T(8,128)} %bitcast.19), calls=%async_computation.2 | async-start | bytes 1310720 | tf_op jit(solution)/shard_map/all_to_all | solution.py:160
  117.3 0.2 fusion.7
  117.5 0.6 fusion.4
  118.2 1.9 %collective-permute-start.1 = (f32[320,640]{1,0:T(8,128)S(1)}, f32[320,640]{1,0:T(8,128)S(1)}, u32[]{:S(2)}, u32[]{:S(2)}) collective-permute-start(f32[320,640]{1,0:T(8,128)S(1)} %fusion.4), channel_id=1, source_target_pairs={{0,1},{1,0},{2,3},{3,2},{4,5},{5,4},{6,7},{7,6},{8,9},{9,8},{10,11... | collective-permute-start | bytes 2457608 | tf_op jit(solution)/shard_map/ppermute | solution.py:167
  120.1 0.8 fusion.1
  120.9 2.4 %collective-permute-start.2 = (f32[320,640]{1,0:T(8,128)S(1)}, f32[320,640]{1,0:T(8,128)S(1)}, u32[]{:S(2)}, u32[]{:S(2)}) collective-permute-start(f32[320,640]{1,0:T(8,128)S(1)} %fusion.1), channel_id=1, source_target_pairs={{0,1},{1,0},{2,3},{3,2},{4,5},{5,4},{6,7},{7,6},{8,9},{9,8},{10,11... | collective-permute-start | bytes 2457608 | tf_op jit(solution)/shard_map/ppermute | solution.py:168
  123.3 0.0 collective-permute-done.1
  123.3 1.5 %convolution_add_fusion.1 = f32[320,640]{1,0:T(8,128)} fusion(f32[320,640]{1,0:T(8,128)S(1)} %collective-permute-done.1, f32[256,640]{1,0:T(8,128)S(1)} %bitcast.23, f32[256,640]{1,0:T(8,128)S(1)} %all_gather.3.both_ref), kind=kOutput, calls=%fused_computation.3 | convolution fusion | flops 314777600 | bytes 2686976 | tf_op jit(solution)/shard_map/dot_general | solution.py:28
  124.8 0.4 collective-permute-done.2
  125.2 1.6 %fusion = f32[640,320]{0,1:T(8,128)} fusion(f32[320,640]{1,0:T(8,128)S(1)} %collective-permute-done.2, f32[256,640]{1,0:T(8,128)S(1)} %bitcast.22, f32[256,640]{1,0:T(8,128)S(1)} %all_gather.3.both_ref), kind=kOutput, calls=%fused_computation.2 | convolution fusion | flops 314777600 | bytes 2686976 | tf_op jit(solution)/shard_map/dot_general | solution.py:28
  126.9 11.7 %all-to-all-done.2.parts_ref = f32[16,16,640]{2,1,0:T(8,128)} async-done(((f32[16,16,640]{2,1,0:T(8,128)}), f32[16,16,640]{2,1,0:T(8,128)}, u32[]{:S(2)}, u32[]{:S(2)}) %all-to-all-start.2) | async-done | bytes 655392 | tf_op jit(solution)/shard_map/all_to_all | solution.py:160
  138.5 1.8 %shard_map.78 = (f32[16,320]{1,0:T(8,128)}, f32[16,320]{1,0:T(8,128)}) custom-call(f32[16,16,640]{2,1,0:T(8,128)} %all-to-all-done.2.parts_ref), custom_call_target="tpu_custom_call" | custom-call | tf_op jit(solution)/shard_map/pallas_call | solution.py:66
  (8 shorter events, 0.0 us)
Async XLA Ops:
  0.6 40.6 %copy-start.1 = (f32[640,320]{0,1:T(8,128)S(1)}, f32[640,320]{0,1:T(8,128)}, u32[]{:S(2)}) copy-start(f32[640,320]{0,1:T(8,128)} %param.6) | copy-start | bytes 2457604
  0.6 40.6 %copy-start = (f32[320,640]{1,0:T(8,128)S(1)}, f32[320,640]{1,0:T(8,128)}, u32[]{:S(2)}) copy-start(f32[320,640]{1,0:T(8,128)} %w_in_ref.3) | copy-start | bytes 2457604
  0.7 3.6 %copy-start.3 = (f32[16,320]{1,0:T(8,128)S(1)}, f32[16,320]{1,0:T(8,128)}, u32[]{:S(2)}) copy-start(f32[16,320]{1,0:T(8,128)} %param.7) | copy-start | bytes 61444
  0.7 3.6 %copy-start.4 = (f32[16,320]{1,0:T(8,128)S(1)}, f32[16,320]{1,0:T(8,128)}, u32[]{:S(2)}) copy-start(f32[16,320]{1,0:T(8,128)} %param.4) | copy-start | bytes 61444
  2.3 39.0 %collective-permute-start = (f32[2,320,640]{2,1,0:T(8,128)S(1)}, f32[2,320,640]{2,1,0:T(8,128)S(1)}, u32[]{:S(2)}, u32[]{:S(2)}) collective-permute-start(f32[2,320,640]{2,1,0:T(8,128)S(1)} %pad_maximum_fusion), channel_id=1, source_target_pairs={{0,1},{1,0},{2,3},{3,2},{4,5},{5,4},{6,7},{7,6},{8,9},{9,8},{10,11... | collective-permute-start | bytes 4915208 | tf_op jit(solution)/shard_map/ppermute | solution.py:149
  107.6 0.8 copy-start.2
  108.4 30.1 %all-to-all-start.2 = ((f32[16,16,640]{2,1,0:T(8,128)}), f32[16,16,640]{2,1,0:T(8,128)}, u32[]{:S(2)}, u32[]{:S(2)}) async-start(f32[16,16,640]{2,1,0:T(8,128)} %bitcast.19), calls=%async_computation.2 | async-start | bytes 1310720 | tf_op jit(solution)/shard_map/all_to_all | solution.py:160
  118.2 5.1 %collective-permute-start.1 = (f32[320,640]{1,0:T(8,128)S(1)}, f32[320,640]{1,0:T(8,128)S(1)}, u32[]{:S(2)}, u32[]{:S(2)}) collective-permute-start(f32[320,640]{1,0:T(8,128)S(1)} %fusion.4), channel_id=1, source_target_pairs={{0,1},{1,0},{2,3},{3,2},{4,5},{5,4},{6,7},{7,6},{8,9},{9,8},{10,11... | collective-permute-start | bytes 2457608 | tf_op jit(solution)/shard_map/ppermute | solution.py:167
  120.9 4.4 %collective-permute-start.2 = (f32[320,640]{1,0:T(8,128)S(1)}, f32[320,640]{1,0:T(8,128)S(1)}, u32[]{:S(2)}, u32[]{:S(2)}) collective-permute-start(f32[320,640]{1,0:T(8,128)S(1)} %fusion.1), channel_id=1, source_target_pairs={{0,1},{1,0},{2,3},{3,2},{4,5},{5,4},{6,7},{7,6},{8,9},{9,8},{10,11... | collective-permute-start | bytes 2457608 | tf_op jit(solution)/shard_map/ppermute | solution.py:168

commit v4 on v3

--- a/solution.py
+++ b/solution.py
@@ -12,6 +12,9 @@
 SWAP = ((0, 1), (1, 0))
 SIDE, DEPTH = 4, 16
 ROWS = SIDE * SIDE
+ROW_RING = [(i + 5) % ROWS for i in range(ROWS)]
+RING = [(i + 12) % DEPTH for i in range(DEPTH)]
+
 
 def gelu_parts(hidden):
     coeff = math.sqrt(2.0 / math.pi)
@@ -148,16 +151,16 @@
     w_out = w_out.T
     other = lax.ppermute(jnp.stack([w_in, w_out]), "core", SWAP)
 
-    both = lax.all_gather(jnp.concatenate([tokens, out_grad], axis=1), "z", axis=0, tiled=True)
+    both = lax.all_gather(jnp.concatenate([tokens, out_grad], axis=1), "z", axis=0, tiled=True, axis_index_groups=[RING])
 
     shape = floats(ROWS, 2, 2, part, hid)
     sums = local_call(first_body, shape, both, w_in, w_out, other)
-    sums = lax.all_to_all(sums, ROW, 0, 0)
+    sums = lax.all_to_all(sums, ROW, 0, 0, axis_index_groups=[ROW_RING])
 
-    full = lax.all_to_all(local_call(middle_body, shape, sums), ROW, 0, 0)
+    full = lax.all_to_all(local_call(middle_body, shape, sums), ROW, 0, 0, axis_index_groups=[ROW_RING])
 
     res = local_call(second_body, floats(total, 2 * width), full, w_in, w_out, other)
-    res = lax.all_to_all(res.reshape(DEPTH, few, 2 * width), "z", 0, 0)
+    res = lax.all_to_all(res.reshape(DEPTH, few, 2 * width), "z", 0, 0, axis_index_groups=[RING])
 
     acts = [full[:, 0, i].reshape(total, hid) for i in (0, 1)]
     hgs = [full[:, 1, i].reshape(total, hid) for i in (0, 1)]

time: 141 us -> 139 us (0.986)
  the two profiles are of different devices: /device:TPU:32 before, /device:TPU:8 now
where the time goes in v4:
time: 139 us
  blocking collectives  95.8 us (69%)
  starting transfers between devices  14.1 us (10%)
  waiting for transfers between devices  10.4 us (7%)
  Pallas kernels  10.1 us (7%)
  matrix products  4.58 us (3%)
  other arithmetic  1.69 us (1%)
    all_gather x1, blocking collectives, on_device(): lax.all_gather(jnp.concatenate([tokens, out_grad], axis=1), 'z', axis=0,...  39.2 us
    all_to_all x1, blocking collectives, on_device(): sums = lax.all_to_all(sums, ROW, 0, 0, axis_index_groups=[ROW_RING])  32.3 us
    all_to_all x1, blocking collectives, on_device(): lax.all_to_all(local_call(middle_body, shape, sums), ROW, 0, 0, axis_inde...  24.3 us
    pallas_call x4, Pallas kernels, local_call(): pl.pallas_call(body, out_shape=out_shape, in_specs=[pl.BlockSpec(memory_s...  10.1 us
    all_to_all x1, waiting for transfers between devices, on_device(): lax.all_to_all(res.reshape(DEPTH, few, 2 * width), 'z', 0, 0, axis_index_...  9.99 us
    all_to_all x1, starting transfers between devices, on_device(): lax.all_to_all(res.reshape(DEPTH, few, 2 * width), 'z', 0, 0, axis_index_...  7.89 us
    dot_general x4, matrix products, dot(): lax.dot_general(left, right, (((left_dim,), (right_dim,)), ((), ())), pre...  4.58 us
  transfers between devices with their start and end apart: 4, of which 2 were waited for; matrix products, arithmetic and copies ran while one was open for 4% of the time, Pallas kernels for 0%

profile of v4, /device:TPU:8, one launch (start us, length us, event | category | flops | bytes accessed | tf_op | source)
XLA Modules:
  0.0 138.6 jit_solution(16715320732541605064)
XLA Ops:
  0.6 0.0 copy-start.1
  0.7 1.6 %pad_maximum_fusion = f32[2,320,640]{2,1,0:T(8,128)S(1)} fusion(f32[1,320,640]{2,1,0:T(8,128)} %bitcast.16, f32[1,320,640]{2,1,0:T(8,128)} %bitcast.15), kind=kLoop, calls=%fused_computation | loop fusion | flops 409600 | bytes 3276800 | tf_op jit(solution)/shard_map/stack | solution.py:152
  2.3 1.9 %collective-permute-start = (f32[2,320,640]{2,1,0:T(8,128)S(1)}, f32[2,320,640]{2,1,0:T(8,128)S(1)}, u32[]{:S(2)}, u32[]{:S(2)}) collective-permute-start(f32[2,320,640]{2,1,0:T(8,128)S(1)} %pad_maximum_fusion), channel_id=1, source_target_pairs={{0,1},{1,0},{2,3},{3,2},{4,5},{5,4},{6,7},{7,6},{8,9},{9,8},{10,11... | collective-permute-start | bytes 4915208 | tf_op jit(solution)/shard_map/ppermute | solution.py:152
  4.2 0.1 pad_maximum_fusion.1
  4.3 39.2 %all_gather.3.both_ref = f32[256,640]{1,0:T(8,128)S(1)} all-gather(f32[16,640]{1,0:T(8,128)S(1)} %pad_maximum_fusion.1), channel_id=1, replica_groups={{24,26,28,30,0,2,4,6,8,10,12,14,16,18,20,22},{25,27,29,31,1,3,5,7,9,11,..., dimensions={0}, use_global_device_ids=true | all-gather | bytes 696320 | tf_op jit(solution)/shard_map/all_gather | solution.py:154
  43.5 0.0 collective-permute-done.other_ref
  43.6 6.4 %shard_map.75 = f32[16,2,2,16,640]{4,3,2,1,0:T(8,128)S(1)} custom-call(f32[256,640]{1,0:T(8,128)S(1)} %all_gather.3.both_ref, f32[320,640]{1,0:T(8,128)S(1)} %copy-done, f32[320,640]{1,0:T(8,128)S(1)} %bitcast.17, f32[2,320,640]{2,1,0:T(8,128)S(1)} %collective-permute-done.other_ref), custom_call_target="tpu_custom_call" | custom-call | tf_op jit(solution)/shard_map/pallas_call | solution.py:69
  49.9 32.3 %all_to_all.15.parts_ref = f32[16,2,2,16,640]{4,3,2,1,0:T(8,128)S(1)} all-to-all(f32[16,2,2,16,640]{4,3,2,1,0:T(8,128)S(1)} %shard_map.75), channel_id=1, replica_groups={{160,192,224,256,288,320,352,384,416,448,480,0,32,64,96,128},{161,193,2..., dimensions={0} | all-to-all | bytes 5242880 | tf_op jit(solution)/shard_map/all_to_all | solution.py:158
  82.2 0.3 shard_map.76
  82.5 24.3 %all_to_all.16.full_ref = f32[16,2,2,16,640]{4,3,2,1,0:T(8,128)S(1)} all-to-all(f32[16,2,2,16,640]{4,3,2,1,0:T(8,128)S(1)} %shard_map.76), channel_id=1, replica_groups={{160,192,224,256,288,320,352,384,416,448,480,0,32,64,96,128},{161,193,2..., dimensions={0} | all-to-all | bytes 5242880 | tf_op jit(solution)/shard_map/all_to_all | solution.py:160
  106.9 1.6 %shard_map.77 = f32[256,640]{1,0:T(8,128)S(1)} custom-call(f32[16,2,2,16,640]{4,3,2,1,0:T(8,128)S(1)} %all_to_all.16.full_ref, f32[320,640]{1,0:T(8,128)S(1)} %copy-done, f32[320,640]{1,0:T(8,128)S(1)} %bitcast.18, f32[2,320,640]{2,1,0:T(8,128)S(1)} %collective-permute-done.other_ref), custom_call_target="tpu_custom_call" | custom-call | tf_op jit(solution)/shard_map/pallas_call | solution.py:69
  108.5 0.8 copy-done.2
  109.3 7.9 %all-to-all-start.2 = ((f32[16,16,640]{2,1,0:T(8,128)}), f32[16,16,640]{2,1,0:T(8,128)}, u32[]{:S(2)}, u32[]{:S(2)}) async-start(f32[16,16,640]{2,1,0:T(8,128)} %bitcast.19), calls=%async_computation.2 | async-start | bytes 1310720 | tf_op jit(solution)/shard_map/all_to_all | solution.py:163
  117.2 0.2 fusion.7
  117.5 0.6 fusion.4
  118.1 1.9 %collective-permute-start.1 = (f32[320,640]{1,0:T(8,128)S(1)}, f32[320,640]{1,0:T(8,128)S(1)}, u32[]{:S(2)}, u32[]{:S(2)}) collective-permute-start(f32[320,640]{1,0:T(8,128)S(1)} %fusion.4), channel_id=1, source_target_pairs={{0,1},{1,0},{2,3},{3,2},{4,5},{5,4},{6,7},{7,6},{8,9},{9,8},{10,11... | collective-permute-start | bytes 2457608 | tf_op jit(solution)/shard_map/ppermute | solution.py:170
  120.0 0.8 fusion.1
  120.8 2.4 %collective-permute-start.2 = (f32[320,640]{1,0:T(8,128)S(1)}, f32[320,640]{1,0:T(8,128)S(1)}, u32[]{:S(2)}, u32[]{:S(2)}) collective-permute-start(f32[320,640]{1,0:T(8,128)S(1)} %fusion.1), channel_id=1, source_target_pairs={{0,1},{1,0},{2,3},{3,2},{4,5},{5,4},{6,7},{7,6},{8,9},{9,8},{10,11... | collective-permute-start | bytes 2457608 | tf_op jit(solution)/shard_map/ppermute | solution.py:171
  123.2 0.0 collective-permute-done.1
  123.2 1.5 %convolution_add_fusion.1 = f32[320,640]{1,0:T(8,128)} fusion(f32[320,640]{1,0:T(8,128)S(1)} %collective-permute-done.1, f32[256,640]{1,0:T(8,128)S(1)} %bitcast.23, f32[256,640]{1,0:T(8,128)S(1)} %all_gather.3.both_ref), kind=kOutput, calls=%fused_computation.3 | convolution fusion | flops 314777600 | bytes 2686976 | tf_op jit(solution)/shard_map/dot_general | solution.py:31
  124.8 0.4 collective-permute-done.2
  125.2 1.6 %fusion = f32[640,320]{0,1:T(8,128)} fusion(f32[320,640]{1,0:T(8,128)S(1)} %collective-permute-done.2, f32[256,640]{1,0:T(8,128)S(1)} %bitcast.22, f32[256,640]{1,0:T(8,128)S(1)} %all_gather.3.both_ref), kind=kOutput, calls=%fused_computation.2 | convolution fusion | flops 314777600 | bytes 2686976 | tf_op jit(solution)/shard_map/dot_general | solution.py:31
  126.8 10.0 %all-to-all-done.2.parts_ref = f32[16,16,640]{2,1,0:T(8,128)} async-done(((f32[16,16,640]{2,1,0:T(8,128)}), f32[16,16,640]{2,1,0:T(8,128)}, u32[]{:S(2)}, u32[]{:S(2)}) %all-to-all-start.2) | async-done | bytes 655392 | tf_op jit(solution)/shard_map/all_to_all | solution.py:163
  136.8 1.8 %shard_map.78 = (f32[16,320]{1,0:T(8,128)}, f32[16,320]{1,0:T(8,128)}) custom-call(f32[16,16,640]{2,1,0:T(8,128)} %all-to-all-done.2.parts_ref), custom_call_target="tpu_custom_call" | custom-call | tf_op jit(solution)/shard_map/pallas_call | solution.py:69
  (8 shorter events, 0.0 us)
Async XLA Ops:
  0.6 42.9 %copy-start.1 = (f32[640,320]{0,1:T(8,128)S(1)}, f32[640,320]{0,1:T(8,128)}, u32[]{:S(2)}) copy-start(f32[640,320]{0,1:T(8,128)} %param.6) | copy-start | bytes 2457604
  0.6 42.9 %copy-start = (f32[320,640]{1,0:T(8,128)S(1)}, f32[320,640]{1,0:T(8,128)}, u32[]{:S(2)}) copy-start(f32[320,640]{1,0:T(8,128)} %w_in_ref.3) | copy-start | bytes 2457604
  0.7 3.6 %copy-start.3 = (f32[16,320]{1,0:T(8,128)S(1)}, f32[16,320]{1,0:T(8,128)}, u32[]{:S(2)}) copy-start(f32[16,320]{1,0:T(8,128)} %param.7) | copy-start | bytes 61444
  0.7 3.6 %copy-start.4 = (f32[16,320]{1,0:T(8,128)S(1)}, f32[16,320]{1,0:T(8,128)}, u32[]{:S(2)}) copy-start(f32[16,320]{1,0:T(8,128)} %param.4) | copy-start | bytes 61444
  2.3 41.3 %collective-permute-start = (f32[2,320,640]{2,1,0:T(8,128)S(1)}, f32[2,320,640]{2,1,0:T(8,128)S(1)}, u32[]{:S(2)}, u32[]{:S(2)}) collective-permute-start(f32[2,320,640]{2,1,0:T(8,128)S(1)} %pad_maximum_fusion), channel_id=1, source_target_pairs={{0,1},{1,0},{2,3},{3,2},{4,5},{5,4},{6,7},{7,6},{8,9},{9,8},{10,11... | collective-permute-start | bytes 4915208 | tf_op jit(solution)/shard_map/ppermute | solution.py:152
  108.5 0.8 copy-start.2
  109.3 27.5 %all-to-all-start.2 = ((f32[16,16,640]{2,1,0:T(8,128)}), f32[16,16,640]{2,1,0:T(8,128)}, u32[]{:S(2)}, u32[]{:S(2)}) async-start(f32[16,16,640]{2,1,0:T(8,128)} %bitcast.19), calls=%async_computation.2 | async-start | bytes 1310720 | tf_op jit(solution)/shard_map/all_to_all | solution.py:163
  118.1 5.1 %collective-permute-start.1 = (f32[320,640]{1,0:T(8,128)S(1)}, f32[320,640]{1,0:T(8,128)S(1)}, u32[]{:S(2)}, u32[]{:S(2)}) collective-permute-start(f32[320,640]{1,0:T(8,128)S(1)} %fusion.4), channel_id=1, source_target_pairs={{0,1},{1,0},{2,3},{3,2},{4,5},{5,4},{6,7},{7,6},{8,9},{9,8},{10,11... | collective-permute-start | bytes 2457608 | tf_op jit(solution)/shard_map/ppermute | solution.py:170
  120.8 4.4 %collective-permute-start.2 = (f32[320,640]{1,0:T(8,128)S(1)}, f32[320,640]{1,0:T(8,128)S(1)}, u32[]{:S(2)}, u32[]{:S(2)}) collective-permute-start(f32[320,640]{1,0:T(8,128)S(1)} %fusion.1), channel_id=1, source_target_pairs={{0,1},{1,0},{2,3},{3,2},{4,5},{5,4},{6,7},{7,6},{8,9},{9,8},{10,11... | collective-permute-start | bytes 2457608 | tf_op jit(solution)/shard_map/ppermute | solution.py:171

commit v5 on v4

--- a/solution.py
+++ b/solution.py
@@ -14,6 +14,8 @@
 ROWS = SIDE * SIDE
 ROW_RING = [(i + 5) % ROWS for i in range(ROWS)]
 RING = [(i + 12) % DEPTH for i in range(DEPTH)]
+
+PAIRS = [(2 * z + c, 2 * ((z + (1 if z % 2 == c else -1)) % DEPTH) + c) for z in range(DEPTH) for c in (0, 1)]
 
 
 def gelu_parts(hidden):
@@ -112,8 +114,9 @@
         mine_ref[i, 1] = hgrad
 
 
-def second_body(full_ref, w_in_ref, w_out_ref, other_ref, res_ref):
-    total = res_ref.shape[0]
+def second_body(full_ref, w_in_ref, w_out_ref, other_ref, keep_ref, send_ref):
+    n, few, _ = keep_ref.shape
+    total = 2 * n * few
     hid = w_in_ref.shape[1]
 
     def product(which, w_ref):
@@ -126,7 +129,10 @@
             preferred_element_type=jnp.float32,
         )
 
-    res_ref[...] = jnp.concatenate([product(0, w_out_ref), product(1, w_in_ref)], axis=0).T
+    res = jnp.concatenate([product(0, w_out_ref), product(1, w_in_ref)], axis=0).T.reshape(n, 2, few, -1)
+    odd = lax.axis_index("z") % 2 == 1
+    keep_ref[...] = jnp.where(odd, res[:, 1], res[:, 0])
+    send_ref[...] = jnp.where(odd, res[:, 0], res[:, 1])
 
 
 def last_body(parts_ref, output_ref, in_grad_ref):
@@ -159,8 +165,10 @@
 
     full = lax.all_to_all(local_call(middle_body, shape, sums), ROW, 0, 0, axis_index_groups=[ROW_RING])
 
-    res = local_call(second_body, floats(total, 2 * width), full, w_in, w_out, other)
-    res = lax.all_to_all(res.reshape(DEPTH, few, 2 * width), "z", 0, 0, axis_index_groups=[RING])
+    block = floats(DEPTH // 2, few, 2 * width)
+    keep, send = local_call(second_body, (block, block), full, w_in, w_out, other)
+    res = keep + lax.ppermute(send, COL, PAIRS)
+    res = lax.all_to_all(res, "z", 0, 0, axis_index_groups=[RING[0::2], RING[1::2]])
 
     acts = [full[:, 0, i].reshape(total, hid) for i in (0, 1)]
     hgs = [full[:, 1, i].reshape(total, hid) for i in (0, 1)]

time: 139 us -> 145 us (1.043)
  waiting for transfers between devices: 10.4 us -> 14.2 us
  matrix products: 4.58 us -> 6.51 us
    ppermute x0 -> x1, waiting for transfers between devices: none -> 3.39 us  [on_device(): res = keep + lax.ppermute(send, COL, PAIRS)]
    dot_general x4, matrix products: 4.58 us -> 6.51 us  [dot(): lax.dot_general(left, right, (((left_dim,), (right_dim,)), ((), ())), pre...]
    ppermute x0 -> x1, starting transfers between devices: none -> 1.92 us  [on_device(): res = keep + lax.ppermute(send, COL, PAIRS)]
  transfers between devices with their start and end apart: 4 -> 5, of which waited for: 2 -> 2; matrix products, arithmetic and copies ran while one was open for 4% -> 5% of each run, Pallas kernels for 0% -> 0%
where the time goes in v5:
time: 145 us
  blocking collectives  95.8 us (66%)
  starting transfers between devices  15.5 us (11%)
  waiting for transfers between devices  14.2 us (10%)
  Pallas kernels  9.01 us (6%)
  matrix products  6.51 us (4%)
  other arithmetic  2.46 us (2%)
    all_gather x1, blocking collectives, on_device(): lax.all_gather(jnp.concatenate([tokens, out_grad], axis=1), 'z', axis=0,...  39.2 us
    all_to_all x1, blocking collectives, on_device(): sums = lax.all_to_all(sums, ROW, 0, 0, axis_index_groups=[ROW_RING])  32.3 us
    all_to_all x1, blocking collectives, on_device(): lax.all_to_all(local_call(middle_body, shape, sums), ROW, 0, 0, axis_inde...  24.3 us
    all_to_all x1, waiting for transfers between devices, on_device(): lax.all_to_all(res, 'z', 0, 0, axis_index_groups=[RING[0::2], RING[1::2]])  10.8 us
    pallas_call x4, Pallas kernels, local_call(): pl.pallas_call(body, out_shape=out_shape, in_specs=[pl.BlockSpec(memory_s...  9.01 us
    all_to_all x1, starting transfers between devices, on_device(): lax.all_to_all(res, 'z', 0, 0, axis_index_groups=[RING[0::2], RING[1::2]])  7.83 us
    dot_general x4, matrix products, dot(): lax.dot_general(left, right, (((left_dim,), (right_dim,)), ((), ())), pre...  6.51 us
    ppermute x1, waiting for transfers between devices, on_device(): res = keep + lax.ppermute(send, COL, PAIRS)  3.39 us
  transfers between devices with their start and end apart: 5, of which 2 were waited for; matrix products, arithmetic and copies ran while one was open for 5% of the time, Pallas kernels for 0%

profile of v5, /device:TPU:8, one launch (start us, length us, event | category | flops | bytes accessed | tf_op | source)
XLA Modules:
  0.0 144.5 jit_solution(10973213838948457530)
XLA Ops:
  0.7 1.6 %pad_maximum_fusion = f32[2,320,640]{2,1,0:T(8,128)S(1)} fusion(f32[1,320,640]{2,1,0:T(8,128)} %bitcast.15, f32[1,320,640]{2,1,0:T(8,128)} %bitcast.14), kind=kLoop, calls=%fused_computation | loop fusion | flops 409600 | bytes 3276800 | tf_op jit(solution)/shard_map/stack | solution.py:158
  2.3 1.9 %collective-permute-start = (f32[2,320,640]{2,1,0:T(8,128)S(1)}, f32[2,320,640]{2,1,0:T(8,128)S(1)}, u32[]{:S(2)}, u32[]{:S(2)}) collective-permute-start(f32[2,320,640]{2,1,0:T(8,128)S(1)} %pad_maximum_fusion), channel_id=1, source_target_pairs={{0,1},{1,0},{2,3},{3,2},{4,5},{5,4},{6,7},{7,6},{8,9},{9,8},{10,11... | collective-permute-start | bytes 4915208 | tf_op jit(solution)/shard_map/ppermute | solution.py:158
  4.2 0.1 pad_maximum_fusion.1
  4.3 39.2 %all_gather.3.both_ref = f32[256,640]{1,0:T(8,128)S(1)} all-gather(f32[16,640]{1,0:T(8,128)S(1)} %pad_maximum_fusion.1), channel_id=1, replica_groups={{24,26,28,30,0,2,4,6,8,10,12,14,16,18,20,22},{25,27,29,31,1,3,5,7,9,11,..., dimensions={0}, use_global_device_ids=true | all-gather | bytes 696320 | tf_op jit(solution)/shard_map/all_gather | solution.py:160
  43.5 0.0 collective-permute-done.other_ref
  43.6 6.4 %shard_map.75 = f32[16,2,2,16,640]{4,3,2,1,0:T(8,128)S(1)} custom-call(f32[256,640]{1,0:T(8,128)S(1)} %all_gather.3.both_ref, f32[320,640]{1,0:T(8,128)S(1)} %copy-done, f32[320,640]{1,0:T(8,128)S(1)} %bitcast.16, f32[2,320,640]{2,1,0:T(8,128)S(1)} %collective-permute-done.other_ref), custom_call_target="tpu_custom_call" | custom-call | tf_op jit(solution)/shard_map/pallas_call | solution.py:71
  49.9 32.3 %all_to_all.15.parts_ref = f32[16,2,2,16,640]{4,3,2,1,0:T(8,128)S(1)} all-to-all(f32[16,2,2,16,640]{4,3,2,1,0:T(8,128)S(1)} %shard_map.75), channel_id=1, replica_groups={{160,192,224,256,288,320,352,384,416,448,480,0,32,64,96,128},{161,193,2..., dimensions={0} | all-to-all | bytes 5242880 | tf_op jit(solution)/shard_map/all_to_all | solution.py:164
  82.2 0.3 shard_map.76
  82.5 24.3 %all_to_all.16.full_ref = f32[16,2,2,16,640]{4,3,2,1,0:T(8,128)S(1)} all-to-all(f32[16,2,2,16,640]{4,3,2,1,0:T(8,128)S(1)} %shard_map.76), channel_id=1, replica_groups={{160,192,224,256,288,320,352,384,416,448,480,0,32,64,96,128},{161,193,2..., dimensions={0} | all-to-all | bytes 5242880 | tf_op jit(solution)/shard_map/all_to_all | solution.py:166
  106.9 1.6 %shard_map.77 = (f32[8,16,640]{2,1,0:T(8,128)S(1)}, f32[8,16,640]{2,1,0:T(8,128)S(1)}) custom-call(f32[16,2,2,16,640]{4,3,2,1,0:T(8,128)S(1)} %all_to_all.16.full_ref, f32[320,640]{1,0:T(8,128)S(1)} %copy-done, f32[320,640]{1,0:T(8,128)S(1)} %bitcast.17, f32[2,320,640]{2,1,0:T(8,128)S(1)} %collective-permute-done.other_ref), custom_call_target="tpu_custom_call" | custom-call | tf_op jit(solution)/shard_map/pallas_call | solution.py:71
  108.5 1.9 %collective-permute-start.1 = (f32[8,16,640]{2,1,0:T(8,128)S(1)}, f32[8,16,640]{2,1,0:T(8,128)S(1)}, u32[]{:S(2)}, u32[]{:S(2)}) collective-permute-start(f32[8,16,640]{2,1,0:T(8,128)S(1)} %get-tuple-element.9), channel_id=1, source_target_pairs={{0,2},{1,31},{2,0},{3,5},{4,6},{5,3},{6,4},{7,9},{8,10},{9,7},{10,... | collective-permute-start | bytes 983048 | tf_op jit(solution)/shard_map/ppermute | solution.py:170
  110.4 0.2 fusion.7
  110.6 1.5 %fusion.4 = f32[320,640]{1,0:T(8,128)} fusion(f32[256,640]{1,0:T(8,128)S(1)} %bitcast.19, f32[256,640]{1,0:T(8,128)S(1)} %all_gather.3.both_ref), kind=kOutput, calls=%fused_computation.7 | convolution fusion | flops 314572800 | bytes 1867776 | tf_op jit(solution)/shard_map/dot_general | solution.py:33
  112.1 1.9 %collective-permute-start.2 = (f32[320,640]{1,0:T(8,128)}, f32[320,640]{1,0:T(8,128)}, u32[]{:S(2)}, u32[]{:S(2)}) collective-permute-start(f32[320,640]{1,0:T(8,128)} %fusion.4), channel_id=1, source_target_pairs={{0,1},{1,0},{2,3},{3,2},{4,5},{5,4},{6,7},{7,6},{8,9},{9,8},{10,11... | collective-permute-start | bytes 2457608 | tf_op jit(solution)/shard_map/ppermute | solution.py:178
  114.1 3.4 %collective-permute-done.1 = f32[8,16,640]{2,1,0:T(8,128)S(1)} collective-permute-done((f32[8,16,640]{2,1,0:T(8,128)S(1)}, f32[8,16,640]{2,1,0:T(8,128)S(1)}, u32[]{:S(2)}, u32[]{:S(2)}) %collective-permute-start.1) | collective-permute-done | bytes 327712 | tf_op jit(solution)/shard_map/ppermute | solution.py:170
  117.5 0.8 add.9
  118.2 7.8 %all-to-all-start.2 = ((f32[8,16,640]{2,1,0:T(8,128)}), f32[8,16,640]{2,1,0:T(8,128)S(1)}, u32[]{:S(2)}, u32[]{:S(2)}) async-start(f32[8,16,640]{2,1,0:T(8,128)} %add.9), calls=%async_computation.2 | async-start | bytes 655360 | tf_op jit(solution)/shard_map/all_to_all | solution.py:171
  126.1 0.7 fusion.1
  126.8 1.9 %collective-permute-start.3 = (f32[320,640]{1,0:T(8,128)S(1)}, f32[320,640]{1,0:T(8,128)S(1)}, u32[]{:S(2)}, u32[]{:S(2)}) collective-permute-start(f32[320,640]{1,0:T(8,128)S(1)} %fusion.1), channel_id=1, source_target_pairs={{0,1},{1,0},{2,3},{3,2},{4,5},{5,4},{6,7},{7,6},{8,9},{9,8},{10,11... | collective-permute-start | bytes 2457608 | tf_op jit(solution)/shard_map/ppermute | solution.py:179
  128.7 0.0 collective-permute-done.2
  128.7 2.6 %convolution_add_fusion.1 = f32[320,640]{1,0:T(8,128)} fusion(f32[320,640]{1,0:T(8,128)} %collective-permute-done.2, f32[256,640]{1,0:T(8,128)S(1)} %bitcast.21, f32[256,640]{1,0:T(8,128)S(1)} %all_gather.3.both_ref), kind=kOutput, calls=%fused_computation.3 | convolution fusion | flops 314777600 | bytes 2686976 | tf_op jit(solution)/shard_map/dot_general | solution.py:33
  131.4 1.6 %fusion = f32[640,320]{0,1:T(8,128)} fusion(f32[320,640]{1,0:T(8,128)S(1)} %collective-permute-done.3, f32[256,640]{1,0:T(8,128)S(1)} %bitcast.20, f32[256,640]{1,0:T(8,128)S(1)} %all_gather.3.both_ref), kind=kOutput, calls=%fused_computation.2 | convolution fusion | flops 314777600 | bytes 2686976 | tf_op jit(solution)/shard_map/dot_general | solution.py:33
  133.0 10.8 %all-to-all-done.2.parts_ref = f32[8,16,640]{2,1,0:T(8,128)S(1)} async-done(((f32[8,16,640]{2,1,0:T(8,128)}), f32[8,16,640]{2,1,0:T(8,128)S(1)}, u32[]{:S(2)}, u32[]{:S(2)}) %all-to-all-start.2) | async-done | bytes 327712 | tf_op jit(solution)/shard_map/all_to_all | solution.py:171
  143.8 0.7 shard_map.78
  (9 shorter events, 0.0 us)
Async XLA Ops:
  0.6 42.9 %copy-start.1 = (f32[640,320]{0,1:T(8,128)S(1)}, f32[640,320]{0,1:T(8,128)}, u32[]{:S(2)}) copy-start(f32[640,320]{0,1:T(8,128)} %param.6) | copy-start | bytes 2457604
  0.6 42.9 %copy-start = (f32[320,640]{1,0:T(8,128)S(1)}, f32[320,640]{1,0:T(8,128)}, u32[]{:S(2)}) copy-start(f32[320,640]{1,0:T(8,128)} %w_in_ref.3) | copy-start | bytes 2457604
  0.7 3.6 %copy-start.2 = (f32[16,320]{1,0:T(8,128)S(1)}, f32[16,320]{1,0:T(8,128)}, u32[]{:S(2)}) copy-start(f32[16,320]{1,0:T(8,128)} %param.7) | copy-start | bytes 61444
  0.7 3.6 %copy-start.3 = (f32[16,320]{1,0:T(8,128)S(1)}, f32[16,320]{1,0:T(8,128)}, u32[]{:S(2)}) copy-start(f32[16,320]{1,0:T(8,128)} %param.4) | copy-start | bytes 61444
  2.3 41.3 %collective-permute-start = (f32[2,320,640]{2,1,0:T(8,128)S(1)}, f32[2,320,640]{2,1,0:T(8,128)S(1)}, u32[]{:S(2)}, u32[]{:S(2)}) collective-permute-start(f32[2,320,640]{2,1,0:T(8,128)S(1)} %pad_maximum_fusion), channel_id=1, source_target_pairs={{0,1},{1,0},{2,3},{3,2},{4,5},{5,4},{6,7},{7,6},{8,9},{9,8},{10,11... | collective-permute-start | bytes 4915208 | tf_op jit(solution)/shard_map/ppermute | solution.py:158
  108.5 9.0 %collective-permute-start.1 = (f32[8,16,640]{2,1,0:T(8,128)S(1)}, f32[8,16,640]{2,1,0:T(8,128)S(1)}, u32[]{:S(2)}, u32[]{:S(2)}) collective-permute-start(f32[8,16,640]{2,1,0:T(8,128)S(1)} %get-tuple-element.9), channel_id=1, source_target_pairs={{0,2},{1,31},{2,0},{3,5},{4,6},{5,3},{6,4},{7,9},{8,10},{9,7},{10,... | collective-permute-start | bytes 983048 | tf_op jit(solution)/shard_map/ppermute | solution.py:170
  112.1 16.6 %collective-permute-start.2 = (f32[320,640]{1,0:T(8,128)}, f32[320,640]{1,0:T(8,128)}, u32[]{:S(2)}, u32[]{:S(2)}) collective-permute-start(f32[320,640]{1,0:T(8,128)} %fusion.4), channel_id=1, source_target_pairs={{0,1},{1,0},{2,3},{3,2},{4,5},{5,4},{6,7},{7,6},{8,9},{9,8},{10,11... | collective-permute-start | bytes 2457608 | tf_op jit(solution)/shard_map/ppermute | solution.py:178
  118.2 25.6 %all-to-all-start.2 = ((f32[8,16,640]{2,1,0:T(8,128)}), f32[8,16,640]{2,1,0:T(8,128)S(1)}, u32[]{:S(2)}, u32[]{:S(2)}) async-start(f32[8,16,640]{2,1,0:T(8,128)} %add.9), calls=%async_computation.2 | async-start | bytes 655360 | tf_op jit(solution)/shard_map/all_to_all | solution.py:171
  126.8 4.6 %collective-permute-start.3 = (f32[320,640]{1,0:T(8,128)S(1)}, f32[320,640]{1,0:T(8,128)S(1)}, u32[]{:S(2)}, u32[]{:S(2)}) collective-permute-start(f32[320,640]{1,0:T(8,128)S(1)} %fusion.1), channel_id=1, source_target_pairs={{0,1},{1,0},{2,3},{3,2},{4,5},{5,4},{6,7},{7,6},{8,9},{9,8},{10,11... | collective-permute-start | bytes 2457608 | tf_op jit(solution)/shard_map/ppermute | solution.py:179
